TPU v7x, 256 devices: a whole 4x4x8 slice. The times are simulated.
256 devices in a mesh: seq: 32 (over z, y_hi, core), dp: 8 (over x, y_lo).
Axes of the slice: x: 4, y: 4 (y_hi: 2, y_lo: 2; y = y_hi * 2 + y_lo), z: 8, core: 2. Of those that a mesh axis runs over, the one named last changes fastest.
Arguments:
- queries: bfloat16 [8, 4096, 3072], P('dp', 'seq'), may hold values from -9 to 9
- keys: bfloat16 [8, 4096, 512], P('dp', 'seq'), may hold values from -6 to 6
- values: bfloat16 [8, 4096, 512], P('dp', 'seq'), may hold values from -6 to 6
- stretch_ids: int32 [8, 4096], P('dp'), may hold values from 0 to 63, never falling along the last dimension, each value on 1 to 256 neighbouring positions
- residual_in: bfloat16 [8, 4096, 6144], P(None, 'seq', 'dp'), may hold values from -6 to 6
- out_proj: bfloat16 [3072, 6144], P(None, 'dp'), may hold values from -0.875 to 0.875
- proj_in: bfloat16 [6144, 1024], P('dp'), may hold values from -0.078125 to 0.078125
- proj_out: bfloat16 [1024, 1536], replicated, may hold values from -0.1875 to 0.1875
- teacher_store: bfloat16 [8, 32, 256, 1536], P('dp', 'seq'), may hold values from -6 to 6
- reader_map: int32 [8, 4096, 1], P('dp', 'seq'), may hold values from 0 to 31; in each aligned block of 128 rows (0 to 127, 128 to 255, ..., all dimensions but the last counted through in order) at most 8 rows name the same one
Outputs:
- alignment: float32 [8, 4096], P('dp', 'seq')
- grad_proj_out: float32 [1024, 1536], P(('seq', 'dp'))
Inputs may be any that keep to these rules, and one draw needn't show every extreme that they name: `stretch_ids`: along each clip the stretch number never falls; each stretch holds 1 to 256 tokens and some stretch holds exactly 256. `reader_map`: within each aligned block of 128 tokens (the tokens of one device) no reader is named more than 8 times, a bound that some block reaches; every reader is named somewhere.
All inputs are finite; a program needn't handle non-finite values.
Results may differ from a plain program's by a relative error of at most 0.024.
Values may be sent and summed in bfloat16 or wider, within the bound.
No kernel may reach another device: no remote copies, remote signals or barrier semaphores. Data moves between devices by JAX's collectives and lax.ppermute only.
A program may use at most 128 MiB of HBM per device.

v0:
```python
import jax
import jax.numpy as jnp
from jax import lax
from jax.sharding import PartitionSpec as P

HD = 128
HEADS = 24
GROUPS = 4


NEG = -1e30
EPS = 1e-06


def attend_block(state, query, stretch_query, key_rows, value_rows, stretch_keys):
    highest, total, accum = state
    count = key_rows.shape[0]
    key_heads = key_rows.reshape(count, GROUPS, HD)
    value_heads = value_rows.reshape(count, GROUPS, HD)
    scores = jnp.einsum(
        "tgrd,pgd->tgrp", query, key_heads, preferred_element_type=jnp.float32
    ) * HD ** (-0.5)
    visible = stretch_keys[None, :] <= stretch_query[:, None]
    scores = jnp.where(visible[:, None, None, :], scores, NEG)
    new_high = jnp.maximum(highest, jnp.max(scores, axis=-1))
    factor = jnp.exp(highest - new_high)
    weights = jnp.exp(scores - new_high[..., None])
    total = total * factor + jnp.sum(weights, axis=-1)
    accum = accum * factor[..., None] + jnp.einsum(
        "tgrp,pgd->tgrd",
        weights.astype(jnp.bfloat16),
        value_heads,
        preferred_element_type=jnp.float32,
    )
    return (new_high, total, accum)


def attend_one(state, query, stretch_query, key_rows, value_rows, stretch_keys):
    return attend_block(state, query, stretch_query, key_rows, value_rows, stretch_keys)


def attend_piece(state, query, stretch_query, key_rows, value_rows, stretch_keys):
    count = key_rows.shape[0]
    span = 512
    parts = count // span

    def advance(inner, pieces):
        key_part, value_part, stretch_part = pieces
        return (attend_one(inner, query, stretch_query, key_part, value_part, stretch_part), None)

    state, _ = lax.scan(
        advance,
        state,
        (
            key_rows.reshape(parts, span, key_rows.shape[1]),
            value_rows.reshape(parts, span, value_rows.shape[1]),
            stretch_keys.reshape(parts, span),
        ),
    )
    return state


def align(projected, target):
    proj_square = jnp.sum(projected * projected, axis=-1) + EPS
    target_square = jnp.sum(target * target, axis=-1) + EPS
    inner = jnp.sum(projected * target, axis=-1)
    denominator = jnp.sqrt(proj_square * target_square)
    cosine = inner / denominator
    grad_rows = -(target / denominator[:, None] - (cosine / proj_square)[:, None] * projected)
    return (cosine, grad_rows)


def on_device(
    queries,
    keys,
    values,
    stretch_ids,
    residual_in,
    out_proj,
    proj_in,
    proj_out,
    teacher_store,
    reader_map,
):
    rows_here = queries.shape[1]
    per_group = HEADS // GROUPS
    place = lax.axis_index("seq")
    seq_count = lax.axis_size("seq")
    stretch_row = stretch_ids[0]
    query_rows = queries[0]
    stretch_query = lax.dynamic_slice_in_dim(stretch_row, place * rows_here, rows_here)
    query = query_rows.reshape(rows_here, GROUPS, per_group, HD)
    state = (
        jnp.full((rows_here, GROUPS, per_group), NEG, jnp.float32),
        jnp.zeros((rows_here, GROUPS, per_group), jnp.float32),
        jnp.zeros((rows_here, GROUPS, per_group, HD), jnp.float32),
    )
    key_piece = lax.all_gather(keys[0], "seq", axis=0, tiled=True)
    value_piece = lax.all_gather(values[0], "seq", axis=0, tiled=True)
    state = attend_piece(state, query, stretch_query, key_piece, value_piece, stretch_row)
    highest, total, accum = state
    attended = (accum / total[..., None]).reshape(rows_here, HEADS * HD).astype(jnp.bfloat16)
    gathered = lax.all_gather(attended, "dp", axis=0, tiled=True)
    clips_here = residual_in.shape[0]
    residual = residual_in.reshape(clips_here * rows_here, residual_in.shape[2])
    hidden = (
        residual.astype(jnp.float32)
        + jnp.dot(gathered, out_proj, preferred_element_type=jnp.float32)
    ).astype(jnp.bfloat16)
    pre = lax.psum_scatter(
        jnp.dot(hidden, proj_in, preferred_element_type=jnp.float32).astype(jnp.bfloat16),
        "dp",
        scatter_dimension=0,
        tiled=True,
    ).astype(jnp.float32)
    act = jax.nn.silu(pre).astype(jnp.bfloat16)
    projected = jnp.dot(act, proj_out, preferred_element_type=jnp.float32)
    slots = teacher_store.shape[2] // seq_count
    store = teacher_store.reshape(seq_count, slots, teacher_store.shape[3])
    arrived = lax.all_to_all(store, "seq", split_axis=0, concat_axis=0, tiled=True)
    readers = reader_map[0, :, 0]
    onehot = (readers[:, None] == jnp.arange(seq_count, dtype=jnp.int32)[None, :]).astype(jnp.int32)
    before = jnp.cumsum(onehot, axis=0) - onehot
    rank = jnp.sum(before * onehot, axis=1)
    target = jnp.take(
        arrived.reshape(seq_count * slots, arrived.shape[2]), readers * slots + rank, axis=0
    ).astype(jnp.float32)
    cosine, grad_rows = align(projected, target)
    delta = grad_rows.astype(jnp.bfloat16)
    grads = lax.psum_scatter(
        jnp.dot(act.T, delta, preferred_element_type=jnp.float32),
        ("seq", "dp"),
        scatter_dimension=0,
        tiled=True,
    )
    return (cosine.reshape(1, rows_here), grads)


def solution(mesh):
    return jax.shard_map(
        on_device,
        mesh=mesh,
        in_specs=(
            P("dp", "seq", None),
            P("dp", "seq", None),
            P("dp", "seq", None),
            P("dp", None),
            P(None, "seq", "dp"),
            P(None, "dp"),
            P("dp", None),
            P(),
            P("dp", "seq", None, None),
            P("dp", "seq", None),
        ),
        out_specs=(P("dp", "seq"), P(("seq", "dp"), None)),
        check_vma=False,
    )
```

profile of v0, /device:TPU:2, one launch (start us, length us, event | category | flops | bytes accessed | tf_op | source)
XLA Modules:
  0.0 862.0 jit_solution(15771031286234748532)
XLA Ops:
  15.9 84.7 %all-gather.8.cloned.1.call-done = bf16[1,4096,512]{2,1,0:T(8,128)(2,1)} async-done(((bf16[1,128,512]{2,1,0:T(8,128)(2,1)}), bf16[1,4096,512]{2,1,0:T(8,128)(2,1)}) %all-gather.8.cloned.1.call-update) | async-done | bytes 4194320 | tf_op jit(solution)/shard_map/all_gather | solution.py:98
  100.6 86.3 %all-gather.10.cloned.1.call-done = bf16[1,4096,512]{2,1,0:T(8,128)(2,1)} async-done(((bf16[1,128,512]{2,1,0:T(8,128)(2,1)}), bf16[1,4096,512]{2,1,0:T(8,128)(2,1)}) %all-gather.10.cloned.1.call-update) | async-done | bytes 4194320 | tf_op jit(solution)/shard_map/all_gather | solution.py:99
  186.9 175.0 %while.15 = (s32[]{:T(128)}, f32[128,4,6]{0,2,1:T(8,128)S(1)}, f32[128,4,6]{0,2,1:T(8,128)S(1)}, f32[128,4,6,128]{0,3,2,1:T(8,128)}, s32[8,512]{1,0:T(8,128)S(1)...) while((s32[]{:T(128)}, f32[128,4,6]{0,2,1:T(8,128)S(1)}, ...), condition=%wide.region_3.4_spmd.clone, body=%wide.region_0.3_spmd.clone.sunk | while | flops 823868416 | bytes 28514944 | solution.py:51
  191.4 5.1 fusion.52
  202.6 5.8 bitcast_add_fusion.3
  212.9 5.1 fusion.52
  224.1 6.2 bitcast_add_fusion.3
  234.8 5.1 fusion.52
  246.0 6.2 bitcast_add_fusion.3
  256.7 5.1 fusion.52
  268.0 6.2 bitcast_add_fusion.3
  278.6 5.1 fusion.52
  289.9 6.2 bitcast_add_fusion.3
  300.6 5.1 fusion.52
  311.8 6.2 bitcast_add_fusion.3
  322.5 5.1 fusion.52
  333.7 6.2 bitcast_add_fusion.3
  355.6 6.2 bitcast_add_fusion.3
  364.6 128.7 %all-gather.6.cloned.1.call-done = bf16[1024,3072]{0,1:T(8,128)(2,1)} async-done(((bf16[128,3072]{0,1:T(8,128)(2,1)}), bf16[1024,3072]{0,1:T(8,128)(2,1)}) %all-gather.6.cloned.1.call-update) | async-done | bytes 6291472 | tf_op jit(solution)/shard_map/all_gather | solution.py:103
  493.3 16.0 %convolution_convert_fusion = bf16[1024,1024]{1,0:T(8,128)(2,1)} fusion(bf16[768,1024]{1,0:T(8,128)(2,1)} %param.18, bf16[1024,768]{1,0:T(8,128)(2,1)} %bitcast.83, bf16[1024,3072]{0,1:T(8,128)(2,1)} %all-gather.6.cloned.1.call-done, bf16[3072,768]{1,0:T(8,128)(2,1)} %param.17), kind=kOutput, calls=%fused_computation.25 | convolution fusion | flops 6445858816 | bytes 16252928 | tf_op jit(solution)/shard_map/dot_general | solution.py:111
  509.4 10.8 %all-to-all-start = ((bf16[32,8,1536]{2,1,0:T(8,128)(2,1)}), bf16[32,8,1536]{2,1,0:T(8,128)(2,1)}, u32[]{:S(2)}, u32[]{:S(2)}) async-start(bf16[32,8,1536]{2,1,0:T(8,128)(2,1)} %bitcast.79), calls=%async_computation.1 | async-start | bytes 1572864 | tf_op jit(solution)/shard_map/all_to_all | solution.py:120
  520.7 22.9 %all-to-all-done = bf16[32,8,1536]{2,1,0:T(8,128)(2,1)} async-done(((bf16[32,8,1536]{2,1,0:T(8,128)(2,1)}), bf16[32,8,1536]{2,1,0:T(8,128)(2,1)}, u32[]{:S(2)}, u32[]{:S(2)}) %all-to-all-start) | async-done | bytes 786464 | tf_op jit(solution)/shard_map/all_to_all | solution.py:120
  546.1 27.5 %reduce-scatter.2.cloned.1.call-done = bf16[128,1024]{1,0:T(8,128)(2,1)} async-done(((bf16[1024,1024]{1,0:T(8,128)(2,1)}), bf16[128,1024]{1,0:T(8,128)(2,1)}) %reduce-scatter.2.cloned.1.call-update) | async-done | bytes 262160 | tf_op jit(solution)/shard_map/reduce_scatter | solution.py:110
  579.8 274.2 %all-reduce.3.cloned.1.call-done = f32[1024,1536]{1,0:T(8,128)} async-done(((f32[1024,1536]{1,0:T(8,128)}), f32[1024,1536]{1,0:T(8,128)}) %all-reduce.3.cloned.1.call-update) | async-done | bytes 6291472
  (110 shorter events, 111.6 us)
Async XLA Ops:
  7.2 566.5 %copy-start = (bf16[1024,1536]{1,0:T(8,128)(2,1)S(1)}, bf16[1024,1536]{1,0:T(8,128)(2,1)}, u32[]{:S(2)}) copy-start(bf16[1024,1536]{1,0:T(8,128)(2,1)} %param.19) | copy-start | bytes 9437188
  7.2 93.5 %all-gather.8.cloned.1.call-start = ((), (), s32[]{:S(2)}) async-start(), calls=%async_computation.4 | async-start | bytes 4325376 | tf_op jit(solution)/shard_map/all_gather | solution.py:98
  7.9 179.0 %all-gather.10.cloned.1.call-start = ((), (), s32[]{:S(2)}) async-start(), calls=%async_computation.5 | async-start | bytes 4325376 | tf_op jit(solution)/shard_map/all_gather | solution.py:99
  8.7 484.7 %all-gather.6.cloned.1.call-start = ((), (), s32[]{:S(2)}) async-start(), calls=%async_computation.2 | async-start | bytes 7077888 | tf_op jit(solution)/shard_map/all_gather | solution.py:103
  364.4 209.2 %reduce-scatter.2.cloned.1.call-start = ((), (), s32[]{:S(2)}) async-start(), calls=%async_computation.3 | async-start | bytes 2359296 | tf_op jit(solution)/shard_map/reduce_scatter | solution.py:110
  493.3 26.9 %copy-start.2 = (s32[1,128,1]{1,2,0:T(1,128)S(1)}, s32[1,128,1]{1,2,0:T(1,128)}, u32[]{:S(2)}) copy-start(s32[1,128,1]{1,2,0:T(1,128)} %param.21) | copy-start | bytes 1540
  509.4 34.3 %all-to-all-start = ((bf16[32,8,1536]{2,1,0:T(8,128)(2,1)}), bf16[32,8,1536]{2,1,0:T(8,128)(2,1)}, u32[]{:S(2)}, u32[]{:S(2)}) async-start(bf16[32,8,1536]{2,1,0:T(8,128)(2,1)} %bitcast.79), calls=%async_computation.1 | async-start | bytes 1572864 | tf_op jit(solution)/shard_map/all_to_all | solution.py:120
  520.2 333.9 %all-reduce.3.cloned.1.call-start = ((), (), s32[]{:S(2)}) async-start(), calls=%async_computation.6 | async-start | bytes 12582912
  573.6 2.3 copy-start.1
Sparse Core Ops, SparseCore 0:
  10.8 89.7 all-gather.7
  103.4 83.4 all-gather.9
  364.5 128.7 all-gather.5
  509.5 64.0 reduce-scatter.1
  579.9 274.0 all-reduce.2
where the time goes:
time: 864 us; the launch traced here: 862 us
  waiting for transfers between devices  626 us (72%)
  matrix products  112 us (13%)
  local copies, waits for them, and re-layouts  60.5 us (7%)
  other arithmetic  38.6 us (4%)
  between operations  13.9 us (2%)
  starting transfers between devices  11.2 us (1%)
    unnamed x6, waiting for transfers between devices  276 us
    all_gather x1, waiting for transfers between devices, on_device(): gathered = lax.all_gather(attended, 'dp', axis=0, tiled=True)  129 us
    all_gather x1, waiting for transfers between devices, on_device(): value_piece = lax.all_gather(values[0], 'seq', axis=0, tiled=True)  86.3 us
    all_gather x1, waiting for transfers between devices, on_device(): key_piece = lax.all_gather(keys[0], 'seq', axis=0, tiled=True)  84.7 us
    dynamic_slice x32, local copies, waits for them, and re-layouts, attend_piece(): lax.scan(advance, state, (key_rows.reshape(parts, span, key_rows.shape[1]...  50.8 us
    dot_general x8, matrix products, attend_block(): jnp.einsum('tgrp,pgd->tgrd', weights.astype(jnp.bfloat16), value_heads, p...  49.5 us
    dot_general x8, matrix products, attend_block(): jnp.einsum('tgrd,pgd->tgrp', query, key_heads, preferred_element_type=jnp...  40.7 us
    reduce_sum x8, other arithmetic, attend_block(): total = total * factor + jnp.sum(weights, axis=-1)  32.5 us
  transfers between devices with their start and end apart: 6, of which 6 were waited for; matrix products, arithmetic and copies ran while one was open for 1% of the time, Pallas kernels for 0%

commit v1 on v0

v1 whole, which is shorter than its diff:
```python
import functools

import jax
import jax.numpy as jnp
from jax import lax
from jax.experimental import pallas as pl
from jax.experimental.pallas import tpu as pltpu
from jax.sharding import Mesh, PartitionSpec as P

HD = 128
HEADS = 24
GROUPS = 4
PER = HEADS // GROUPS
NEG = -1e30
EPS = 1e-06
SCALE2 = HD ** (-0.5) * 1.4426950408889634

AXES = ("z", "yh", "core", "x", "yl")
SIZES = (8, 2, 2, 4, 2)
SEQ = ("z", "yh", "core")
DP = ("x", "yl")
QUAD = ("yh", "core")


def flash_kernel(n, first, last, meta, q_ref, c_ref, *refs):
    kv = refs[:n]
    refs = refs[n:]
    if not first:
        m_in, l_in, a_in = refs[:3]
        refs = refs[3:]
    if last:
        out, m_ref, l_ref, a_ref = refs[:4]
        vt = refs[4:]
    else:
        m_ref, l_ref, a_ref = refs[:3]
        vt = refs[3:]

    @pl.when(pl.program_id(0) == 0)
    def _():
        for j in range(n):
            vt[j][...] = kv[j][:, HD:].T

    if first:
        m_ref[...] = jnp.full(m_ref.shape, NEG, jnp.float32)
        l_ref[...] = jnp.zeros(l_ref.shape, jnp.float32)
        a_ref[...] = jnp.zeros(a_ref.shape, jnp.float32)
    else:
        m_ref[...] = m_in[...]
        l_ref[...] = l_in[...]
        a_ref[...] = a_in[...]
    lowest = meta[n]
    highest = meta[n + 1]
    for j in range(n):
        base = meta[j]
        rows = kv[j].shape[0]

        def step(masked, j=j, base=base, rows=rows):
            s = jnp.dot(kv[j][:, :HD], q_ref[...], preferred_element_type=jnp.float32)
            if masked:
                place = lax.broadcasted_iota(jnp.int32, s.shape, 0)
                s = jnp.where(place < c_ref[...] - base, s, NEG)
            old = m_ref[0]
            new = jnp.maximum(old, jnp.max(s, axis=0, keepdims=True))
            p = jnp.exp2((s - new) * SCALE2)
            factor = jnp.exp2((old - new) * SCALE2)
            m_ref[0] = new
            l_ref[0] = l_ref[0] * factor + jnp.sum(p, axis=0, keepdims=True)
            a_ref[...] = a_ref[...] * factor + jnp.dot(
                vt[j][...], p.astype(jnp.bfloat16), preferred_element_type=jnp.float32
            )

        whole = base + rows <= lowest

        @pl.when(whole)
        def _(step=step):
            step(False)

        @pl.when(jnp.logical_and(jnp.logical_not(whole), base < highest))
        def _(step=step):
            step(True)

    if last:
        out[...] = (a_ref[...] / l_ref[0]).astype(out.dtype)


def flash(q_t, counts, bounds, pieces, bases, state, last):
    n = len(pieces)
    tokens = q_t.shape[1]
    first = state is None
    meta = jnp.concatenate([jnp.stack(bases).astype(jnp.int32), bounds])
    row = pl.BlockSpec((1, 1, tokens), lambda h, meta: (h, 0, 0))
    head = pl.BlockSpec((HD, tokens), lambda h, meta: (h, 0))
    f32 = jnp.float32
    in_specs = [head, pl.BlockSpec((1, tokens), lambda h, meta: (0, 0))]
    in_specs += [pl.BlockSpec(p.shape, lambda h, meta: (0, 0)) for p in pieces]
    args = [q_t, counts] + list(pieces)
    if not first:
        in_specs += [row, row, head]
        args += list(state)
    scratch = [pltpu.VMEM((HD, p.shape[0]), jnp.bfloat16) for p in pieces]
    if last:
        out_specs = head
        out_shape = jax.ShapeDtypeStruct((PER * HD, tokens), jnp.bfloat16)
        scratch = [
            pltpu.VMEM((1, 1, tokens), f32),
            pltpu.VMEM((1, 1, tokens), f32),
            pltpu.VMEM((HD, tokens), f32),
        ] + scratch
    else:
        out_specs = [row, row, head]
        out_shape = [
            jax.ShapeDtypeStruct((PER, 1, tokens), f32),
            jax.ShapeDtypeStruct((PER, 1, tokens), f32),
            jax.ShapeDtypeStruct((PER * HD, tokens), f32),
        ]
    keys = sum(p.shape[0] for p in pieces)
    return pl.pallas_call(
        functools.partial(flash_kernel, n, first, last),
        grid_spec=pltpu.PrefetchScalarGridSpec(
            num_scalar_prefetch=1,
            grid=(PER,),
            in_specs=in_specs,
            out_specs=out_specs,
            scratch_shapes=scratch,
        ),
        out_shape=out_shape,
        compiler_params=pltpu.CompilerParams(vmem_limit_bytes=32 * 1024 * 1024),
        cost_estimate=pl.CostEstimate(
            flops=4 * PER * tokens * keys * HD,
            bytes_accessed=6 * PER * HD * tokens,
            transcendentals=PER * tokens * keys,
        ),
    )(meta, *args)


def shift(v, k):
    return lax.ppermute(v, "z", [(i, (i + k) % 8) for i in range(8)])


def align(projected, target):
    proj_square = jnp.sum(projected * projected, axis=-1) + EPS
    target_square = jnp.sum(target * target, axis=-1) + EPS
    inner = jnp.sum(projected * target, axis=-1)
    denominator = jnp.sqrt(proj_square * target_square)
    cosine = inner / denominator
    grad_rows = -(target / denominator[:, None] - (cosine / proj_square)[:, None] * projected)
    return (cosine, grad_rows)


def on_device(
    queries,
    keys,
    values,
    stretch_ids,
    residual_in,
    out_proj,
    proj_in,
    proj_out,
    teacher_store,
    reader_map,
):
    f32, bf16 = jnp.float32, jnp.bfloat16
    z = lax.axis_index("z")
    group = lax.axis_index(QUAD)
    core = lax.axis_index("core")
    rows = queries.shape[1]
    tokens = rows * 4

    kv = jnp.concatenate([keys[0].reshape(rows, GROUPS, HD), values[0].reshape(rows, GROUPS, HD)], axis=-1)
    kv = lax.all_to_all(kv.transpose(1, 0, 2), QUAD, 0, 0, tiled=True).reshape(tokens, 2 * HD)
    q = queries[0].reshape(rows, GROUPS, PER * HD).transpose(1, 0, 2)
    q = lax.all_to_all(q, QUAD, 0, 0, tiled=True).reshape(tokens, PER * HD)
    q_t = q.T

    wide = PER * HD // 8
    wo = lax.dynamic_slice_in_dim(out_proj, group * PER * HD + z * wide, wide)
    w = jnp.dot(wo, proj_in, preferred_element_type=f32).astype(bf16)
    w = lax.all_to_all(w.reshape(wide, 8, HD).transpose(1, 0, 2), DP, 0, 0, tiled=True)
    w = jnp.sum(w.astype(f32), axis=0).astype(bf16)
    w = lax.all_gather(w, "z", axis=0, tiled=True)
    w = lax.all_gather(w, DP, axis=0, tiled=False)

    clips = residual_in.shape[0]
    res = jnp.dot(
        residual_in.reshape(clips * rows, residual_in.shape[2]), proj_in, preferred_element_type=f32
    ).astype(bf16)
    res = lax.all_to_all(res.reshape(clips, rows, res.shape[1]), DP, 0, 0, tiled=True)
    res = jnp.sum(res.astype(f32), axis=0)

    store = teacher_store.reshape(32, 8, teacher_store.shape[3])
    arrived = lax.all_to_all(store, SEQ, 0, 0, tiled=True).reshape(256, store.shape[2])
    readers = reader_map[0, :, 0]
    onehot = (readers[:, None] == jnp.arange(32, dtype=jnp.int32)[None, :]).astype(jnp.int32)
    before = jnp.cumsum(onehot, axis=0) - onehot
    rank = jnp.sum(before * onehot, axis=1)
    pick = (readers * 8 + rank)[:, None] == jnp.arange(256, dtype=jnp.int32)[None, :]
    target = jnp.dot(pick.astype(bf16), arrived, preferred_element_type=f32)

    stretch = stretch_ids[0]
    mine = lax.dynamic_slice_in_dim(stretch, z * tokens, tokens)
    counts = jnp.sum((stretch[:, None] <= mine[None, :]).astype(jnp.int32), axis=0)
    bounds = jnp.stack([counts[0], counts[-1]])
    counts = counts[None, :]

    def base(k):
        return lax.rem(z + k + 8, 8) * tokens

    state = flash(q_t, counts, bounds, [kv], [base(0)], None, False)
    fore = back = kv
    for s in range(1, 4):
        fore, back = shift(fore, 1), shift(back, -1)
        state = flash(q_t, counts, bounds, [fore, back], [base(-s), base(s)], state, False)
    half = tokens // 2
    fore, back = shift(fore[:half], 1), shift(back[half:], -1)
    att = flash(q_t, counts, bounds, [fore, back], [base(4), base(4) + half], state, True)

    part = lax.dot_general(att, w, (((0,), (1,)), ((), ())), preferred_element_type=f32)
    part = part.reshape(4, rows, 8 * HD).astype(bf16)
    part = lax.all_to_all(part, QUAD, 0, 0, tiled=True)
    pre = jnp.sum(part.astype(f32), axis=0) + res
    act = jax.nn.silu(pre).astype(bf16)
    projected = jnp.dot(act, proj_out, preferred_element_type=f32)
    cosine, grad_rows = align(projected, target)
    delta = grad_rows.astype(bf16)

    at = jnp.arange(512, dtype=jnp.int32)
    column = (
        (at // 4 % 8) * 128 + (at // 256) * 64 + (at // 64 % 4) * 8 + (at // 32 % 2) * 4 + at % 4
    )

    def chosen(c):
        take = (column + c * 32)[:, None] == jnp.arange(1024, dtype=jnp.int32)[None, :]
        return lax.dot_general(
            take.astype(bf16), act, (((1,), (1,)), ((), ())), preferred_element_type=f32
        ).astype(bf16)

    swap = [(0, 1), (1, 0)]
    other_act = lax.ppermute(chosen(1 - core), "core", swap)
    other_delta = lax.ppermute(delta, "core", swap)
    grads = jnp.dot(chosen(core), delta, preferred_element_type=f32) + jnp.dot(
        other_act, other_delta, preferred_element_type=f32
    )
    grads = grads.astype(bf16).reshape(16, 32, grads.shape[1])
    grads = lax.all_to_all(grads, ("yh", "x", "yl"), 0, 0, tiled=True)
    grads = jnp.sum(grads.astype(f32), axis=0).reshape(8, 4, grads.shape[2])
    grads = jnp.sum(lax.all_to_all(grads, "z", 0, 0, tiled=True), axis=0)
    return (cosine.reshape(1, rows), grads)


def solution(mesh):
    fine = Mesh(mesh.devices.reshape(SIZES), AXES)
    return jax.shard_map(
        on_device,
        mesh=fine,
        in_specs=(
            P(DP, SEQ, None),
            P(DP, SEQ, None),
            P(DP, SEQ, None),
            P(DP, None),
            P(None, SEQ, DP),
            P(None, DP),
            P(DP, None),
            P(),
            P(DP, SEQ, None, None),
            P(DP, SEQ, None),
        ),
        out_specs=(P(DP, SEQ), P(SEQ + DP, None)),
        check_vma=False,
    )
```

time: 864 us -> 267 us (0.31)
  waiting for transfers between devices: 626 us -> 24.2 us
  blocking collectives: 0 us -> 106 us
  matrix products: 112 us -> 20.5 us
  local copies, waits for them, and re-layouts: 60.5 us -> 13.7 us
  starting transfers between devices: 11.2 us -> 52.2 us
  other arithmetic: 38.6 us -> 19.9 us
  Pallas kernels: 0 us -> 13.8 us
    all_gather x3 -> x1, waiting for transfers between devices: 300 us -> 1.37 us  [on_device(): w = lax.all_gather(w, DP, axis=0, tiled=False)]
    unnamed x6 -> x1, waiting for transfers between devices: 276 us -> 0.02 us
    dot_general x19 -> x8, matrix products: 112 us -> 20.5 us  [the longest x1 4.99 us: on_device(): jnp.dot(residual_in.reshape(clips * rows, residual_in.shape[2]), proj_in,...]
    all_to_all x0 -> x3, blocking collectives: none -> 66.3 us  [the longest x1 24.8 us: on_device(): grads = lax.all_to_all(grads, ('yh', 'x', 'yl'), 0, 0, tiled=True)]
    dynamic_slice x33 -> x1, local copies, waits for them, and re-layouts: 51.4 us -> 0.01 us  [on_device(): mine = lax.dynamic_slice_in_dim(stretch, z * tokens, tokens)]
    all_gather x0 -> x1, blocking collectives: none -> 40.1 us  [on_device(): w = lax.all_gather(w, 'z', axis=0, tiled=True)]
    reduce_scatter x1 -> x0, waiting for transfers between devices: 27.5 us -> none  [on_device(): lax.psum_scatter(jnp.dot(hidden, proj_in, preferred_element_type=jnp.floa...]
    reduce_sum x8 -> x6, other arithmetic: 32.5 us -> 7.15 us  [the longest x1 2.81 us: on_device(): res = jnp.sum(res.astype(f32), axis=0)]
  transfers between devices with their start and end apart: 6 -> 16, of which waited for: 6 -> 7; matrix products, arithmetic and copies ran while one was open for 1% -> 15% of each run, Pallas kernels for 0% -> 5%
where the time goes in v1:
time: 267 us; the launch traced here: 265 us
  blocking collectives  106 us (40%)
  starting transfers between devices  52.2 us (20%)
  waiting for transfers between devices  24.2 us (9%)
  matrix products  20.5 us (8%)
  other arithmetic  19.9 us (7%)
  between operations  14.3 us (5%)
  Pallas kernels  13.8 us (5%)
  local copies, waits for them, and re-layouts  13.7 us (5%)
    all_gather x1, blocking collectives, on_device(): w = lax.all_gather(w, 'z', axis=0, tiled=True)  40.1 us
    all_to_all x1, blocking collectives, on_device(): grads = lax.all_to_all(grads, ('yh', 'x', 'yl'), 0, 0, tiled=True)  24.8 us
    all_to_all x1, blocking collectives, on_device(): grads = jnp.sum(lax.all_to_all(grads, 'z', 0, 0, tiled=True), axis=0)  24.1 us
    ppermute x8, starting transfers between devices, shift(): return lax.ppermute(v, 'z', [(i, (i + k) % 8) for i in range(8)])  22.1 us
    all_to_all x1, blocking collectives, on_device(): q = lax.all_to_all(q, QUAD, 0, 0, tiled=True).reshape(tokens, PER * HD)  17.4 us
    pallas_call x5, Pallas kernels, flash(): pl.pallas_call(functools.partial(flash_kernel, n, first, last), grid_spec...  13.8 us
    all_to_all x1, waiting for transfers between devices, on_device(): part = lax.all_to_all(part, QUAD, 0, 0, tiled=True)  10.9 us
    all_to_all x1, starting transfers between devices, on_device(): lax.all_to_all(store, SEQ, 0, 0, tiled=True).reshape(256, store.shape[2])  8.97 us
  transfers between devices with their start and end apart: 16, of which 7 were waited for; matrix products, arithmetic and copies ran while one was open for 15% of the time, Pallas kernels for 5%

profile of v1, /device:TPU:2, one launch (start us, length us, event | category | flops | bytes accessed | tf_op | source)
XLA Modules:
  0.0 264.9 jit_solution(480526389000100747)
XLA Ops:
  9.9 5.8 %all-to-all-start.2 = ((bf16[8,96,128]{2,1,0:T(8,128)(2,1)}), bf16[8,96,128]{2,1,0:T(8,128)(2,1)S(1)}, u32[]{:S(2)}, u32[]{:S(2)}) async-start(bf16[8,96,128]{2,1,0:T(8,128)(2,1)} %bitcast.71), calls=%async_computation.2 | async-start | bytes 393216 | tf_op jit(solution)/shard_map/all_to_all | solution.py:178
  21.6 4.2 %all-to-all-start.1 = ((bf16[4,128,256]{2,1,0:T(8,128)(2,1)}), bf16[4,128,256]{2,1,0:T(8,128)(2,1)S(1)}, u32[]{:S(2)}, u32[]{:S(2)}) async-start(bf16[4,128,256]{2,1,0:T(8,128)(2,1)} %maximum_bitcast_fusion), calls=%async_computation.1 | async-start | bytes 524288 | tf_op jit(solution)/shard_map/all_to_all | solution.py:170
  28.1 5.2 %all-to-all-done.1 = bf16[4,128,256]{2,1,0:T(8,128)(2,1)S(1)} async-done(((bf16[4,128,256]{2,1,0:T(8,128)(2,1)}), bf16[4,128,256]{2,1,0:T(8,128)(2,1)S(1)}, u32[]{:S(2)}, u32[]{:S(2)}) %all-to-all-start.1) | async-done | bytes 262176 | tf_op jit(solution)/shard_map/all_to_all | solution.py:170
  33.3 17.4 %all_to_all.40 = bf16[4,128,768]{1,2,0:T(8,128)(2,1)} all-to-all(bf16[4,128,768]{1,2,0:T(8,128)(2,1)} %bitcast.68), channel_id=1, replica_groups=mesh['z'=8,'yh'=2,'core'=2,'x'=4,'yl'=2] {'yh','core'}, dimensions={0} | all-to-all | bytes 1572864 | tf_op jit(solution)/shard_map/all_to_all | solution.py:172
  50.7 9.0 %all-to-all-start.5 = ((bf16[32,8,1536]{2,1,0:T(8,128)(2,1)}), bf16[32,8,1536]{2,1,0:T(8,128)(2,1)}, u32[]{:S(2)}, u32[]{:S(2)}) async-start(bf16[32,8,1536]{2,1,0:T(8,128)(2,1)} %bitcast.70), calls=%async_computation.5 | async-start | bytes 1572864 | tf_op jit(solution)/shard_map/all_to_all | solution.py:191
  60.7 40.1 %all_gather.9 = bf16[768,128]{1,0:T(8,128)(2,1)} all-gather(bf16[96,128]{1,0:T(8,128)(2,1)S(1)} %reduce_sum.94), channel_id=1, replica_groups=mesh['z'=8,'yh'=2,'core'=2,'x'=4,'yl'=2] {'z'}, dimensions={0}, use_global_device_ids=true | all-gather | bytes 221184 | tf_op jit(solution)/shard_map/all_gather | solution.py:180
  106.3 5.0 %convolution_convert_fusion = bf16[1024,1024]{1,0:T(8,128)(2,1)} fusion(bf16[1024,768]{1,0:T(8,128)(2,1)} %bitcast.76, bf16[768,1024]{1,0:T(8,128)(2,1)} %param.16), kind=kOutput, calls=%fused_computation.10 | convolution fusion | flops 1611661312 | bytes 5242880 | tf_op jit(solution)/shard_map/dot_general | solution.py:184
  111.3 5.9 %all-to-all-start.4 = ((bf16[8,128,1024]{2,1,0:T(8,128)(2,1)}), bf16[8,128,1024]{2,1,0:T(8,128)(2,1)}, u32[]{:S(2)}, u32[]{:S(2)}) async-start(bf16[8,128,1024]{2,1,0:T(8,128)(2,1)} %bitcast.69), calls=%async_computation.4 | async-start | bytes 4194304 | tf_op jit(solution)/shard_map/all_to_all | solution.py:187
  118.6 2.4 collective-permute-start
  125.0 3.8 %collective-permute-done.refs_0_ = bf16[512,256]{1,0:T(8,128)(2,1)} collective-permute-done((bf16[512,256]{1,0:T(8,128)(2,1)S(1)}, bf16[512,256]{1,0:T(8,128)(2,1)}, u32[]{:S(2)}, u32[]{:S(2)}) %collective-permute-start) | collective-permute-done | bytes 262176 | tf_op jit(solution)/shard_map/ppermute | solution.py:137
  128.8 3.4 %collective-permute-start.5 = (bf16[512,256]{1,0:T(8,128)(2,1)}, bf16[512,256]{1,0:T(8,128)(2,1)S(1)}, u32[]{:S(2)}, u32[]{:S(2)}) collective-permute-start(bf16[512,256]{1,0:T(8,128)(2,1)} %collective-permute-done.4.refs_1_), channel_id=1, source_target_pairs={{0,224},{32,0},{64,32},{96,64},{128,96},{160,128},{192,160},{224,1... | collective-permute-start | bytes 786440 | tf_op jit(solution)/shard_map/ppermute | solution.py:137
  133.5 4.8 %shard_map.113 = (f32[6,1,512]{2,1,0:T(1,128)S(1)}, f32[6,1,512]{2,1,0:T(1,128)S(1)}, f32[768,512]{1,0:T(8,128)S(1)}) custom-call(s32[3]{0:T(128)S(1)} %pad_add_fusion.meta, bf16[768,512]{1,0:T(8,128)(2,1)S(1)} %bitcast_bitcast_fusion.q_ref, s32[1,512]{1,0:T(1,128)S(1)} %bitcast.62, bf16[512,256]{1,0:T(8,128)(2,1)S(1)} %bitcast.61), custom_call_target="tpu_custom_call" | custom-call | flops 805306368 | bytes 2359296 | tf_op jit(solution)/shard_map/pallas_call | solution.py:117
  138.4 3.4 %collective-permute-start.6 = (bf16[512,256]{1,0:T(8,128)(2,1)S(1)}, bf16[512,256]{1,0:T(8,128)(2,1)S(1)}, u32[]{:S(2)}, u32[]{:S(2)}) collective-permute-start(bf16[512,256]{1,0:T(8,128)(2,1)S(1)} %collective-permute-done.5.refs_1_), channel_id=1, source_target_pairs={{0,224},{32,0},{64,32},{96,64},{128,96},{160,128},{192,160},{224,1... | collective-permute-start | bytes 786440 | tf_op jit(solution)/shard_map/ppermute | solution.py:137
  141.8 5.9 %shard_map.114 = (f32[6,1,512]{2,1,0:T(1,128)S(1)}, f32[6,1,512]{2,1,0:T(1,128)S(1)}, f32[768,512]{1,0:T(8,128)S(1)}) custom-call(s32[4]{0:T(128)S(1)} %add_add_fusion.3.meta, bf16[768,512]{1,0:T(8,128)(2,1)S(1)} %bitcast_bitcast_fusion.q_ref, s32[1,512]{1,0:T(1,128)S(1)} %bitcast.63, bf16[512,256]{1,0:T(8,128)(2,1)} %collective-permute-done.refs_0_, ...), custom_call_target="tpu_custom_call" | custom-call | flops 1610612736 | bytes 2359296 | tf_op jit(solution)/shard_map/pallas_call | solution.py:117
  148.7 2.9 %collective-permute-start.3 = (bf16[256,256]{1,0:T(8,128)(2,1)S(1)}, bf16[256,256]{1,0:T(8,128)(2,1)S(1)}, u32[]{:S(2)}, u32[]{:S(2)}) collective-permute-start(bf16[256,256]{1,0:T(8,128)(2,1)S(1)} %slice.16), channel_id=1, source_target_pairs={{0,32},{32,64},{64,96},{96,128},{128,160},{160,192},{192,224},{224... | collective-permute-start | bytes 393224 | tf_op jit(solution)/shard_map/ppermute | solution.py:137
  151.7 9.0 %collective-permute-start.7 = (bf16[256,256]{1,0:T(8,128)(2,1)S(1)}, bf16[256,256]{1,0:T(8,128)(2,1)S(1)}, u32[]{:S(2)}, u32[]{:S(2)}) collective-permute-start(bf16[256,256]{1,0:T(8,128)(2,1)S(1)} %slice.17), channel_id=1, source_target_pairs={{0,224},{32,0},{64,32},{96,64},{128,96},{160,128},{192,160},{224,1... | collective-permute-start | bytes 393224 | tf_op jit(solution)/shard_map/ppermute | solution.py:137
  166.8 2.6 %convolution_convert_fusion.1 = bf16[512,8,128]{2,0,1:T(8,128)(2,1)S(1)} fusion(bf16[8,768,128]{2,1,0:T(8,128)(2,1)} %bitcast.77, bf16[768,512]{1,0:T(8,128)(2,1)} %copy-done.1), kind=kOutput, calls=%fused_computation.11 | convolution fusion | flops 805830656 | bytes 3407872 | tf_op jit(solution)/shard_map/dot_general | solution.py:217
  173.5 4.7 %all-to-all-start.3 = ((bf16[4,128,1024]{2,1,0:T(8,128)(2,1)}), bf16[4,128,1024]{2,1,0:T(8,128)(2,1)}, u32[]{:S(2)}, u32[]{:S(2)}) async-start(bf16[4,128,1024]{2,1,0:T(8,128)(2,1)} %convert_element_type.50), calls=%async_computation.3 | async-start | bytes 2097152 | tf_op jit(solution)/shard_map/all_to_all | solution.py:219
  180.6 2.8 %convert_reduce_fusion.1 = f32[128,1024]{1,0:T(8,128)} fusion(bf16[8,128,1024]{2,1,0:T(8,128)(2,1)} %all-to-all-done.4), kind=kLoop, calls=%fused_computation.1 | loop fusion | flops 1966080 | bytes 2621440 | tf_op jit(solution)/shard_map/reduce_sum | solution.py:188
  183.4 10.9 %all-to-all-done.3 = bf16[4,128,1024]{2,1,0:T(8,128)(2,1)} async-done(((bf16[4,128,1024]{2,1,0:T(8,128)(2,1)}), bf16[4,128,1024]{2,1,0:T(8,128)(2,1)}, u32[]{:S(2)}, u32[]{:S(2)}) %all-to-all-start.3) | async-done | bytes 1048608 | tf_op jit(solution)/shard_map/all_to_all | solution.py:219
  200.9 4.0 %fusion.6 = f32[512,1536]{1,0:T(8,128)} fusion(bf16[128,1536]{1,0:T(8,128)(2,1)} %negate_convert_fusion, bf16[128,1024]{1,0:T(8,128)(2,1)S(1)} %multiply_convert_fusion, s32[512]{0:T(512)S(1)} %broadcast_add_fusion.1), kind=kOutput, calls=%fused_computation.16 | convolution fusion | flops 336134144 | bytes 3803136 | tf_op jit(solution)/shard_map/dot_general | solution.py:240
  205.0 2.6 fusion
  207.6 24.8 %all_to_all.41 = bf16[16,32,1536]{2,1,0:T(8,128)(2,1)S(1)} all-to-all(bf16[16,32,1536]{2,1,0:T(8,128)(2,1)S(1)} %bitcast.67), channel_id=1, replica_groups=mesh['z'=8,'yh'=2,'core'=2,'x'=4,'yl'=2] {'yh','x','yl'}, dimensions={0} | all-to-all | bytes 3145728 | tf_op jit(solution)/shard_map/all_to_all | solution.py:244
  233.3 24.1 %all_to_all.42 = f32[8,4,1536]{2,1,0:T(4,128)S(1)} all-to-all(f32[8,4,1536]{2,1,0:T(4,128)} %reshape.193), channel_id=1, replica_groups=mesh['z'=8,'yh'=2,'core'=2,'x'=4,'yl'=2] {'z'}, dimensions={0} | all-to-all | bytes 393216 | tf_op jit(solution)/shard_map/all_to_all | solution.py:246
  (73 shorter events, 45.8 us)
Async XLA Ops:
  7.2 189.9 %copy-start = (bf16[1024,1536]{1,0:T(8,128)(2,1)S(1)}, bf16[1024,1536]{1,0:T(8,128)(2,1)}, u32[]{:S(2)}) copy-start(bf16[1024,1536]{1,0:T(8,128)(2,1)} %param.17) | copy-start | bytes 9437188
  9.9 11.0 %all-to-all-start.2 = ((bf16[8,96,128]{2,1,0:T(8,128)(2,1)}), bf16[8,96,128]{2,1,0:T(8,128)(2,1)S(1)}, u32[]{:S(2)}, u32[]{:S(2)}) async-start(bf16[8,96,128]{2,1,0:T(8,128)(2,1)} %bitcast.71), calls=%async_computation.2 | async-start | bytes 393216 | tf_op jit(solution)/shard_map/all_to_all | solution.py:178
  20.9 0.7 copy-start.3
  21.6 11.7 %all-to-all-start.1 = ((bf16[4,128,256]{2,1,0:T(8,128)(2,1)}), bf16[4,128,256]{2,1,0:T(8,128)(2,1)S(1)}, u32[]{:S(2)}, u32[]{:S(2)}) async-start(bf16[4,128,256]{2,1,0:T(8,128)(2,1)} %maximum_bitcast_fusion), calls=%async_computation.1 | async-start | bytes 524288 | tf_op jit(solution)/shard_map/all_to_all | solution.py:170
  28.1 72.8 %copy-start.5 = (s32[1,4096]{1,0:T(1,128)S(1)}, s32[1,4096]{1,0:T(1,128)}, u32[]{:S(2)}) copy-start(s32[1,4096]{1,0:T(1,128)} %param.13) | copy-start | bytes 49156
  50.7 60.6 %all-to-all-start.5 = ((bf16[32,8,1536]{2,1,0:T(8,128)(2,1)}), bf16[32,8,1536]{2,1,0:T(8,128)(2,1)}, u32[]{:S(2)}, u32[]{:S(2)}) async-start(bf16[32,8,1536]{2,1,0:T(8,128)(2,1)} %bitcast.70), calls=%async_computation.5 | async-start | bytes 1572864 | tf_op jit(solution)/shard_map/all_to_all | solution.py:191
  59.7 107.1 %all-gather.3.cloned.1.call-start = ((), (), s32[]{:S(2)}) async-start(), calls=%async_computation.8 | async-start | bytes 1769472 | tf_op jit(solution)/shard_map/all_gather | solution.py:181
  111.3 7.2 %copy-start.4 = (s32[1,128,1]{1,2,0:T(1,128)S(1)}, s32[1,128,1]{1,2,0:T(1,128)}, u32[]{:S(2)}) copy-start(s32[1,128,1]{1,2,0:T(1,128)} %param.19) | copy-start | bytes 1540
  111.3 62.1 %all-to-all-start.4 = ((bf16[8,128,1024]{2,1,0:T(8,128)(2,1)}), bf16[8,128,1024]{2,1,0:T(8,128)(2,1)}, u32[]{:S(2)}, u32[]{:S(2)}) async-start(bf16[8,128,1024]{2,1,0:T(8,128)(2,1)} %bitcast.69), calls=%async_computation.4 | async-start | bytes 4194304 | tf_op jit(solution)/shard_map/all_to_all | solution.py:187
  118.6 10.2 %collective-permute-start = (bf16[512,256]{1,0:T(8,128)(2,1)S(1)}, bf16[512,256]{1,0:T(8,128)(2,1)}, u32[]{:S(2)}, u32[]{:S(2)}) collective-permute-start(bf16[512,256]{1,0:T(8,128)(2,1)S(1)} %bitcast.59), channel_id=1, source_target_pairs={{0,32},{32,64},{64,96},{96,128},{128,160},{160,192},{192,224},{224... | collective-permute-start | bytes 786440 | tf_op jit(solution)/shard_map/ppermute | solution.py:137
  121.0 7.7 %collective-permute-start.4 = (bf16[512,256]{1,0:T(8,128)(2,1)S(1)}, bf16[512,256]{1,0:T(8,128)(2,1)}, u32[]{:S(2)}, u32[]{:S(2)}) collective-permute-start(bf16[512,256]{1,0:T(8,128)(2,1)S(1)} %bitcast.60), channel_id=1, source_target_pairs={{0,224},{32,0},{64,32},{96,64},{128,96},{160,128},{192,160},{224,1... | collective-permute-start | bytes 786440 | tf_op jit(solution)/shard_map/ppermute | solution.py:137
  128.8 9.5 %collective-permute-start.1 = (bf16[512,256]{1,0:T(8,128)(2,1)}, bf16[512,256]{1,0:T(8,128)(2,1)S(1)}, u32[]{:S(2)}, u32[]{:S(2)}) collective-permute-start(bf16[512,256]{1,0:T(8,128)(2,1)} %collective-permute-done.refs_0_), channel_id=1, source_target_pairs={{0,32},{32,64},{64,96},{96,128},{128,160},{160,192},{192,224},{224... | collective-permute-start | bytes 786440 | tf_op jit(solution)/shard_map/ppermute | solution.py:137
  128.8 9.6 %collective-permute-start.5 = (bf16[512,256]{1,0:T(8,128)(2,1)}, bf16[512,256]{1,0:T(8,128)(2,1)S(1)}, u32[]{:S(2)}, u32[]{:S(2)}) collective-permute-start(bf16[512,256]{1,0:T(8,128)(2,1)} %collective-permute-done.4.refs_1_), channel_id=1, source_target_pairs={{0,224},{32,0},{64,32},{96,64},{128,96},{160,128},{192,160},{224,1... | collective-permute-start | bytes 786440 | tf_op jit(solution)/shard_map/ppermute | solution.py:137
  138.3 10.4 %collective-permute-start.2 = (bf16[512,256]{1,0:T(8,128)(2,1)S(1)}, bf16[512,256]{1,0:T(8,128)(2,1)S(1)}, u32[]{:S(2)}, u32[]{:S(2)}) collective-permute-start(bf16[512,256]{1,0:T(8,128)(2,1)S(1)} %collective-permute-done.1.refs_0_), channel_id=1, source_target_pairs={{0,32},{32,64},{64,96},{96,128},{128,160},{160,192},{192,224},{224... | collective-permute-start | bytes 786440 | tf_op jit(solution)/shard_map/ppermute | solution.py:137
  138.4 13.3 %collective-permute-start.6 = (bf16[512,256]{1,0:T(8,128)(2,1)S(1)}, bf16[512,256]{1,0:T(8,128)(2,1)S(1)}, u32[]{:S(2)}, u32[]{:S(2)}) collective-permute-start(bf16[512,256]{1,0:T(8,128)(2,1)S(1)} %collective-permute-done.5.refs_1_), channel_id=1, source_target_pairs={{0,224},{32,0},{64,32},{96,64},{128,96},{160,128},{192,160},{224,1... | collective-permute-start | bytes 786440 | tf_op jit(solution)/shard_map/ppermute | solution.py:137
  148.7 14.7 %collective-permute-start.3 = (bf16[256,256]{1,0:T(8,128)(2,1)S(1)}, bf16[256,256]{1,0:T(8,128)(2,1)S(1)}, u32[]{:S(2)}, u32[]{:S(2)}) collective-permute-start(bf16[256,256]{1,0:T(8,128)(2,1)S(1)} %slice.16), channel_id=1, source_target_pairs={{0,32},{32,64},{64,96},{96,128},{128,160},{160,192},{192,224},{224... | collective-permute-start | bytes 393224 | tf_op jit(solution)/shard_map/ppermute | solution.py:137
  151.7 11.8 %collective-permute-start.7 = (bf16[256,256]{1,0:T(8,128)(2,1)S(1)}, bf16[256,256]{1,0:T(8,128)(2,1)S(1)}, u32[]{:S(2)}, u32[]{:S(2)}) collective-permute-start(bf16[256,256]{1,0:T(8,128)(2,1)S(1)} %slice.17), channel_id=1, source_target_pairs={{0,224},{32,0},{64,32},{96,64},{128,96},{160,128},{192,160},{224,1... | collective-permute-start | bytes 393224 | tf_op jit(solution)/shard_map/ppermute | solution.py:137
  164.6 0.9 copy-start.1
  173.5 20.8 %all-to-all-start.3 = ((bf16[4,128,1024]{2,1,0:T(8,128)(2,1)}), bf16[4,128,1024]{2,1,0:T(8,128)(2,1)}, u32[]{:S(2)}, u32[]{:S(2)}) async-start(bf16[4,128,1024]{2,1,0:T(8,128)(2,1)} %convert_element_type.50), calls=%async_computation.3 | async-start | bytes 2097152 | tf_op jit(solution)/shard_map/all_to_all | solution.py:219
  194.3 2.7 %copy-start.2 = (f32[128,1536]{1,0:T(8,128)S(1)}, f32[128,1536]{1,0:T(8,128)}, u32[]{:S(2)}) copy-start(f32[128,1536]{1,0:T(8,128)} %fusion.10) | copy-start | bytes 2359300
  199.3 5.7 %collective-permute-start.9 = (bf16[128,1536]{1,0:T(8,128)(2,1)}, bf16[128,1536]{1,0:T(8,128)(2,1)}, u32[]{:S(2)}, u32[]{:S(2)}) collective-permute-start(bf16[128,1536]{1,0:T(8,128)(2,1)} %negate_convert_fusion), channel_id=1, source_target_pairs={{0,8},{8,0},{1,9},{9,1},{2,10},{10,2},{3,11},{11,3},{4,12},{12,4},... | collective-permute-start | bytes 1179656 | tf_op jit(solution)/shard_map/ppermute | solution.py:239
  200.4 4.5 %collective-permute-start.8 = (bf16[512,128]{1,0:T(8,128)(2,1)}, bf16[512,128]{1,0:T(8,128)(2,1)S(1)}, u32[]{:S(2)}, u32[]{:S(2)}) collective-permute-start(bf16[512,128]{1,0:T(8,128)(2,1)} %fusion.3), channel_id=1, source_target_pairs={{0,8},{8,0},{1,9},{9,1},{2,10},{10,2},{3,11},{11,3},{4,12},{12,4},... | collective-permute-start | bytes 393224 | tf_op jit(solution)/shard_map/ppermute | solution.py:238
Sparse Core Ops, SparseCore 0:
  100.9 65.8 all-gather.2
